TPU v7x, 32 devices: a whole 2x2x4 slice. The times are simulated.
32 devices in a mesh: row: 8 (over y, x, core), col: 4 (over z).
Axes of the slice: x: 2, y: 2, z: 4, core: 2. Of those that a mesh axis runs over, the one named last changes fastest.
Arguments:
- density: float32 [1024, 1024], P('row', 'col'), as said below
- pattern: int32 [16, 16], P('row', 'col'), may hold values from 0 to 1, as said below
Outputs:
- purified: float32 [1024, 1024], P('row', 'col')
Inputs may be any that keep to these rules, and one draw needn't show every extreme that they name: pattern is symmetric and its diagonal is 1. density is symmetric and zero in every block where pattern is 0.
All inputs are finite; a program needn't handle non-finite values.
Results may differ from a plain program's by a relative error of at most 0.00013.
Values sent between devices are 32-bit elements; how exact they have to be, the bound alone decides.
A program may use at most 64 MiB of HBM per device.

v0:
```python
import jax
import jax.numpy as jnp
from jax import lax
from jax.sharding import PartitionSpec as P

ITERS = 2


def panel_product(piece, column_stack):
    return jnp.dot(
        piece, column_stack, precision=lax.Precision.HIGHEST, preferred_element_type=jnp.float32
    )


def per_device(density, pattern):
    block_width = density.shape[0] // pattern.shape[0]
    block_mask = jnp.repeat(jnp.repeat(pattern, block_width, axis=0), block_width, axis=1).astype(
        jnp.float32
    )
    current = density
    for step in range(ITERS):
        column_stack = lax.all_gather(current, "row", axis=0, tiled=True)

        def with_current(piece):
            return panel_product(piece, column_stack)

        square = block_mask * with_current(lax.all_gather(current, "col", axis=1, tiled=True))
        cube = block_mask * with_current(lax.all_gather(square, "col", axis=1, tiled=True))
        current = 3.0 * square - 2.0 * cube
    return current


def solution(mesh):
    return jax.shard_map(
        per_device,
        mesh=mesh,
        in_specs=(P("row", "col"), P("row", "col")),
        out_specs=P("row", "col"),
        check_vma=False,
    )
```

profile of v0, /device:TPU:0, one launch (start us, length us, event | category | flops | bytes accessed | tf_op | source)
XLA Modules:
  0.0 105.0 jit_solution(4634129142862879960)
XLA Ops:
  6.5 0.0 all-gather.3.cloned.1.call-start
  6.5 0.7 all-gather.3.cloned.1.call-update
  7.3 0.0 all-gather.5.cloned.1.call-start
  7.3 0.0 copy-done.4
  7.3 0.1 copy.3
  7.4 0.1 broadcast_in_dim.6
  7.5 0.1 convert_element_type.12
  7.6 0.0 copy-start.3
  7.6 0.1 copy.6
  7.7 0.8 copy-done.3
  8.5 17.3 %all_gather.18 = f32[128,1024]{1,0:T(8,128)S(1)} all-gather(f32[128,256]{1,0:T(8,128)S(1)} %copy-done.3), channel_id=1, replica_groups=mesh['row'=8,'col'=4] {'col'}, dimensions={1}, use_global_device_ids=true | all-gather | bytes 655360 | tf_op jit(solution)/shard_map/all_gather | solution.py:27
  25.8 9.6 %all-gather.3.cloned.1.call-done = f32[1024,256]{1,0:T(8,128)} async-done(((f32[128,256]{1,0:T(8,128)}), f32[1024,256]{1,0:T(8,128)}) %all-gather.3.cloned.1.call-update) | async-done | bytes 1048592 | tf_op jit(solution)/shard_map/all_gather | solution.py:22
  35.5 1.9 %convolution_multiply_fusion.3 = f32[128,256]{1,0:T(8,128)S(1)} fusion(f32[128,256]{1,0:T(8,128)S(1)} %copy.6, f32[128,1024]{1,0:T(8,128)S(1)} %all_gather.18, f32[1024,256]{1,0:T(8,128)} %all-gather.3.cloned.1.call-done), kind=kOutput, calls=%fused_computation.7 | convolution fusion | flops 402685952 | bytes 1835008 | tf_op jit(solution)/shard_map/dot_general | solution.py:10
  37.4 16.1 %all_gather.20 = f32[128,1024]{1,0:T(8,128)S(1)} all-gather(f32[128,256]{1,0:T(8,128)S(1)} %convolution_multiply_fusion.3), channel_id=1, replica_groups=mesh['row'=8,'col'=4] {'col'}, dimensions={1}, use_global_device_ids=true | all-gather | bytes 655360 | tf_op jit(solution)/shard_map/all_gather | solution.py:28
  53.5 0.0 copy-done
  53.5 1.3 %fusion.3 = f32[128,256]{1,0:T(8,128)} fusion(f32[128,256]{1,0:T(8,128)S(1)} %copy.6, f32[128,1024]{1,0:T(8,128)S(1)} %all_gather.20, f32[1024,256]{1,0:T(8,128)S(1)} %copy-done, f32[128,256]{1,0:T(8,128)S(1)} %convolution_multiply_fusion.3), kind=kOutput, calls=%fused_computation.6 | convolution fusion | flops 402784256 | bytes 1966080 | tf_op jit(solution)/shard_map/dot_general | solution.py:10
  54.8 0.0 all-gather.5.cloned.1.call-update
  54.8 0.9 copy-done.2
  55.7 16.0 %all_gather.21 = f32[128,1024]{1,0:T(8,128)S(1)} all-gather(f32[128,256]{1,0:T(8,128)S(1)} %copy-done.2), channel_id=1, replica_groups=mesh['row'=8,'col'=4] {'col'}, dimensions={1}, use_global_device_ids=true | all-gather | bytes 655360 | tf_op jit(solution)/shard_map/all_gather | solution.py:27
  71.7 7.2 %all-gather.5.cloned.1.call-done = f32[1024,256]{1,0:T(8,128)} async-done(((f32[128,256]{1,0:T(8,128)}), f32[1024,256]{1,0:T(8,128)}) %all-gather.5.cloned.1.call-update) | async-done | bytes 1048592 | tf_op jit(solution)/shard_map/all_gather | solution.py:22
  78.9 1.9 %convolution_multiply_fusion.1 = f32[128,256]{1,0:T(8,128)S(1)} fusion(f32[128,256]{1,0:T(8,128)S(1)} %copy.6, f32[128,1024]{1,0:T(8,128)S(1)} %all_gather.21, f32[1024,256]{1,0:T(8,128)} %all-gather.5.cloned.1.call-done), kind=kOutput, calls=%fused_computation.3 | convolution fusion | flops 402685952 | bytes 1835008 | tf_op jit(solution)/shard_map/dot_general | solution.py:10
  80.8 16.1 %all_gather.23 = f32[128,1024]{1,0:T(8,128)S(1)} all-gather(f32[128,256]{1,0:T(8,128)S(1)} %convolution_multiply_fusion.1), channel_id=1, replica_groups=mesh['row'=8,'col'=4] {'col'}, dimensions={1}, use_global_device_ids=true | all-gather | bytes 655360 | tf_op jit(solution)/shard_map/all_gather | solution.py:28
  96.9 0.0 copy-done.1
  96.9 1.3 %fusion.1 = f32[128,256]{1,0:T(8,128)} fusion(f32[128,256]{1,0:T(8,128)S(1)} %copy.6, f32[128,1024]{1,0:T(8,128)S(1)} %all_gather.23, f32[1024,256]{1,0:T(8,128)S(1)} %copy-done.1, f32[128,256]{1,0:T(8,128)S(1)} %convolution_multiply_fusion.1), kind=kOutput, calls=%fused_computation.2 | convolution fusion | flops 402784256 | bytes 1966080 | tf_op jit(solution)/shard_map/dot_general | solution.py:10
  (6 shorter events, 0.0 us)
Async XLA Ops:
  6.5 0.8 copy-start.4
  6.5 28.9 %all-gather.3.cloned.1.call-start = ((), (), s32[]{:S(2)}) async-start(), calls=%async_computation | async-start | bytes 1179648 | tf_op jit(solution)/shard_map/all_gather | solution.py:22
  7.3 71.6 %all-gather.5.cloned.1.call-start = ((), (), s32[]{:S(2)}) async-start(), calls=%async_computation.1 | async-start | bytes 1179648 | tf_op jit(solution)/shard_map/all_gather | solution.py:22
  7.6 0.9 copy-start.3
  35.5 18.0 %copy-start = (f32[1024,256]{1,0:T(8,128)S(1)}, f32[1024,256]{1,0:T(8,128)}, u32[]{:S(2)}) copy-start(f32[1024,256]{1,0:T(8,128)} %all-gather.3.cloned.1.call-done) | copy-start | bytes 3145732
  54.8 0.9 copy-start.2
  78.9 18.0 %copy-start.1 = (f32[1024,256]{1,0:T(8,128)S(1)}, f32[1024,256]{1,0:T(8,128)}, u32[]{:S(2)}) copy-start(f32[1024,256]{1,0:T(8,128)} %all-gather.5.cloned.1.call-done) | copy-start | bytes 3145732
Sparse Core Ops, SparseCore 0:
  9.2 26.1 all-gather.2
  54.9 23.8 all-gather.4
where the time goes:
time: 105 us
  blocking collectives  65.5 us (62%)
  waiting for transfers between devices  17.5 us (17%)
  between operations  13.5 us (13%)
  matrix products  6.49 us (6%)
  local copies, waits for them, and re-layouts  2.05 us (2%)
    all_gather x2, blocking collectives, per_device(): lax.all_gather(current, 'col', axis=1, tiled=True)  33.4 us
    all_gather x2, blocking collectives, per_device(): lax.all_gather(square, 'col', axis=1, tiled=True)  32.1 us
    all_gather x2, waiting for transfers between devices, per_device(): column_stack = lax.all_gather(current, 'row', axis=0, tiled=True)  16.8 us
    dot_general x4, matrix products, panel_product(): jnp.dot(piece, column_stack, precision=lax.Precision.HIGHEST, preferred_e...  6.49 us
  transfers between devices with their start and end apart: 2, of which 2 were waited for; matrix products, arithmetic and copies ran while one was open for 0% of the time, Pallas kernels for 0%

commit v1 on v0

v1 whole, which is shorter than its diff:
```python
import functools

import jax
import jax.numpy as jnp
from jax import lax
from jax.experimental import pallas as pl
from jax.experimental.pallas import tpu as pltpu
from jax.sharding import PartitionSpec as P

ITERS = 2
MESH = pl.DeviceIdType.MESH


def split(x):
    high = x.astype(jnp.bfloat16)
    low = (x - high.astype(jnp.float32)).astype(jnp.bfloat16)
    return high, low


def flip(index, mask):
    bit = 1
    while bit <= mask:
        if mask & bit:
            index = index + bit * (1 - 2 * lax.rem(index // bit, 2))
        bit *= 2
    return index


def kernel(nrow, ncol, pattern_ref, density_ref, out_ref, rowp, cols, srow, bh, bl, acc, mask,
           zs, zr, cs, cr, ss, sr):
    h, w = density_ref.shape
    pr, pc = pattern_ref.shape
    plane = nrow // 2
    r, z = lax.axis_index("row"), lax.axis_index("col")
    core = lax.rem(r, 2)
    chip = r // 2
    sib = r + 1 - 2 * core
    zright, zleft = lax.rem(z + 1, ncol), lax.rem(z + ncol - 1, ncol)

    barrier = pltpu.get_barrier_semaphore()
    greet = [(flip(chip, d) * 2 + core, z) for d in range(1, plane)]
    greet += [(sib, z), (r, zright), (r, zleft)]
    for device in greet:
        pl.semaphore_signal(barrier, inc=1, device_id=device, device_id_type=MESH)

    lane_block = lax.broadcasted_iota(jnp.int32, (h // pr, w), 1) // (w // pc)
    for i in range(pr):
        band = jnp.zeros((h // pr, w), jnp.float32)
        for j in range(pc):
            band = jnp.where(lane_block == j, pattern_ref[i, j].astype(jnp.float32), band)
        mask[i * (h // pr):(i + 1) * (h // pr), :] = band

    def rows_of(owner):
        return pl.ds(pl.multiple_of(owner * h, h), h)

    rowp[0, z] = density_ref[...]
    cols[0, rows_of(r), :] = density_ref[...]
    pl.semaphore_wait(barrier, len(greet))

    def remote(ref, send, recv, device):
        return pltpu.make_async_remote_copy(
            src_ref=ref, dst_ref=ref, send_sem=send, recv_sem=recv, device_id=device, device_id_type=MESH)

    def zcopy(buf, ph, way, s, j):
        return remote(buf.at[j], zs.at[ph, way, s], zr.at[ph, way, s], (r, zright if way == 0 else zleft))

    def zstart(buf, ph):
        @pl.when(z < ncol - 1)
        def _():
            zcopy(buf, ph, 0, 0, z).start()

        @pl.when(z > 0)
        def _():
            zcopy(buf, ph, 1, 0, z).start()

    def arrive(buf, ph, s):
        @pl.when(z - s >= 0)
        def _():
            zcopy(buf, ph, 0, s - 1, z - s).wait_recv()

            @pl.when(z < ncol - 1)
            def _():
                zcopy(buf, ph, 0, s, z - s).start()

        @pl.when(z + s <= ncol - 1)
        def _():
            zcopy(buf, ph, 1, s - 1, z + s).wait_recv()

            @pl.when(z > 0)
            def _():
                zcopy(buf, ph, 1, s, z + s).start()

    def zfinish(buf, ph):
        def one(s):
            @pl.when((z - s >= 0) & (z < ncol - 1))
            def _():
                zcopy(buf, ph, 0, s, z - s).wait_send()

            @pl.when((z + s <= ncol - 1) & (z > 0))
            def _():
                zcopy(buf, ph, 1, s, z + s).wait_send()

        over(0, ncol - 1, one)

    def over(low, high, body):
        if ncol <= 4:
            for s in range(low, high):
                body(s)
        else:
            lax.fori_loop(low, high, lambda s, c: (body(s), c)[1], 0)

    def colcopy(it, d, owner, device):
        return remote(cols.at[it, rows_of(owner)], cs.at[it, d], cr.at[it, d], (device, z))

    def sibcopy(it, d, owner):
        return remote(cols.at[it, rows_of(owner)], ss.at[it, d], sr.at[it, d], (sib, z))

    def chunk(buf, it, j, fresh):
        rows = pl.ds(pl.multiple_of(j * w, w), w)
        if fresh:
            bhigh, blow = split(cols[it, rows, :])
            bh[rows, :] = bhigh
            bl[rows, :] = blow
        else:
            bhigh, blow = bh[rows, :], bl[rows, :]
        ahigh, alow = split(buf[j])
        both = jnp.concatenate([ahigh, alow], axis=0)
        p = jnp.dot(both, bhigh, preferred_element_type=jnp.float32)
        q = jnp.dot(ahigh, blow, preferred_element_type=jnp.float32)
        acc[...] += p[:h] + (p[h:] + q)

    def compute(buf, it, s, fresh):
        @pl.when(z - s >= 0)
        def _():
            chunk(buf, it, z - s, fresh)

        @pl.when(z + s <= ncol - 1)
        def _():
            chunk(buf, it, z + s, fresh)

    for it in range(ITERS):
        cur, sq = rowp.at[it], srow.at[it]
        pa, pb = 2 * it, 2 * it + 1
        zstart(cur, pa)
        for d in range(1, plane):
            colcopy(it, d, r, flip(chip, d) * 2 + core).start()
        sibcopy(it, 0, r).start()
        acc[...] = jnp.zeros_like(acc)
        arrive(cur, pa, 1)
        for d in range(1, plane):
            peer = flip(chip, d) * 2 + core
            colcopy(it, d, peer, peer).wait_recv()
            sibcopy(it, d, peer).start()
        arrive(cur, pa, 2)
        for d in range(plane):
            sibcopy(it, d, flip(chip, d) * 2 + 1 - core).wait_recv()
        chunk(cur, it, z, True)
        compute(cur, it, 1, True)
        compute(cur, it, 2, True)

        def finish(s):
            arrive(cur, pa, s)
            compute(cur, it, s, True)

        over(3, ncol, finish)
        square = acc[...] * mask[...]
        sq[z] = square
        zstart(sq, pb)
        acc[...] = jnp.zeros_like(acc)
        chunk(sq, it, z, False)

        def cube(s):
            arrive(sq, pb, s)
            compute(sq, it, s, False)

        over(1, ncol, cube)
        result = 3.0 * sq[z] - 2.0 * (mask[...] * acc[...])
        if it + 1 < ITERS:
            rowp[it + 1, z] = result
            cols[it + 1, rows_of(r), :] = result
        else:
            out_ref[...] = result

    for it in range(ITERS):
        zfinish(rowp.at[it], 2 * it)
        zfinish(srow.at[it], 2 * it + 1)
        for d in range(plane):
            peer = flip(chip, d) * 2 + core
            if d:
                colcopy(it, d, r, peer).wait_send()
            sibcopy(it, d, peer).wait_send()


def solution(mesh):
    nrow, ncol = mesh.shape["row"], mesh.shape["col"]

    def per_device(density, pattern):
        h, w = density.shape
        n = nrow * h
        f32 = jnp.float32
        dma = pltpu.SemaphoreType.DMA
        return pl.pallas_call(
            functools.partial(kernel, nrow, ncol),
            out_shape=jax.ShapeDtypeStruct((h, w), f32),
            in_specs=[pl.BlockSpec(memory_space=pltpu.SMEM), pl.BlockSpec(memory_space=pltpu.VMEM)],
            out_specs=pl.BlockSpec(memory_space=pltpu.VMEM),
            scratch_shapes=[
                pltpu.VMEM((ITERS, ncol, h, w), f32),
                pltpu.VMEM((ITERS, n, w), f32),
                pltpu.VMEM((ITERS, ncol, h, w), f32),
                pltpu.VMEM((n, w), jnp.bfloat16),
                pltpu.VMEM((n, w), jnp.bfloat16),
                pltpu.VMEM((h, w), f32),
                pltpu.VMEM((h, w), f32),
                dma((2 * ITERS, 2, ncol)),
                dma((2 * ITERS, 2, ncol)),
                dma((ITERS, nrow // 2)),
                dma((ITERS, nrow // 2)),
                dma((ITERS, nrow // 2)),
                dma((ITERS, nrow // 2)),
            ],
            compiler_params=pltpu.CompilerParams(
                collective_id=0, has_side_effects=True, vmem_limit_bytes=40 * 1024 * 1024),
            cost_estimate=pl.CostEstimate(
                flops=12 * ITERS * h * n * w, bytes_accessed=8 * h * w, transcendentals=0),
        )(pattern, density)

    return jax.shard_map(
        per_device,
        mesh=mesh,
        in_specs=(P("row", "col"), P("row", "col")),
        out_specs=P("row", "col"),
        check_vma=False,
    )
```

time: 105 us -> 60.9 us (0.58)
  blocking collectives: 65.5 us -> 0 us
  Pallas kernels: 0 us -> 58.5 us
  waiting for transfers between devices: 17.5 us -> 0 us
  between operations: 13.5 us -> 0.01 us
  matrix products: 6.49 us -> 0 us
    all_gather x4 -> x0, blocking collectives: 65.5 us -> none  [the longest x2 33.4 us: per_device(): lax.all_gather(current, 'col', axis=1, tiled=True)]
    pallas_call x0 -> x1, Pallas kernels: none -> 58.5 us  [per_device(): pl.pallas_call(functools.partial(kernel, nrow, ncol), out_shape=jax.Shape...]
    all_gather x2 -> x0, waiting for transfers between devices: 16.8 us -> none  [per_device(): column_stack = lax.all_gather(current, 'row', axis=0, tiled=True)]
    dot_general x4 -> x0, matrix products: 6.49 us -> none  [panel_product(): jnp.dot(piece, column_stack, precision=lax.Precision.HIGHEST, preferred_e...]
    unnamed x10 -> x5, local copies, waits for them, and re-layouts: 1.69 us -> 2.24 us
  transfers between devices with their start and end apart: 2 -> 0, of which waited for: 2 -> 0; matrix products, arithmetic and copies ran while one was open for 0% -> 0% of each run, Pallas kernels for 0% -> 0%
where the time goes in v1:
time: 60.9 us; the launch traced here: 60.7 us
  Pallas kernels  58.5 us (96%)
  local copies, waits for them, and re-layouts  2.24 us (4%)
    pallas_call x1, Pallas kernels, per_device(): pl.pallas_call(functools.partial(kernel, nrow, ncol), out_shape=jax.Shape...  58.5 us
    unnamed x5, local copies, waits for them, and re-layouts  2.24 us

profile of v1, /device:TPU:0, one launch (start us, length us, event | category | flops | bytes accessed | tf_op | source)
XLA Modules:
  0.0 60.7 jit_solution(10266913958016541986)
XLA Ops:
  0.0 0.0 copy-start
  0.0 0.9 %copy-done = f32[128,256]{1,0:T(8,128)S(1)} copy-done((f32[128,256]{1,0:T(8,128)S(1)}, f32[128,256]{1,0:T(8,128)}, u32[]{:S(2)}) %copy-start) | copy-done | bytes 131096
  0.9 0.0 copy-start.1
  0.9 0.7 %copy-done.1 = s32[2,4]{1,0:T(2,128)S(1)} copy-done((s32[2,4]{1,0:T(2,128)S(1)}, s32[2,4]{1,0:T(2,128)}, u32[]{:S(2)}) %copy-start.1) | copy-done | bytes 56
  1.6 58.5 %shard_map.28 = f32[128,256]{1,0:T(8,128)S(1)} custom-call(s32[2,4]{1,0:T(2,128)S(1)} %copy-done.1, f32[128,256]{1,0:T(8,128)S(1)} %copy-done), custom_call_target="tpu_custom_call" | custom-call | flops 805306368 | bytes 262144 | tf_op jit(solution)/shard_map/pallas_call | solution.py:202
  60.1 0.7 %copy.4 = f32[128,256]{1,0:T(8,128)} copy(f32[128,256]{1,0:T(8,128)S(1)} %shard_map.28) | data formatting | bytes 262144
Async XLA Ops:
  0.0 0.9 %copy-start = (f32[128,256]{1,0:T(8,128)S(1)}, f32[128,256]{1,0:T(8,128)}, u32[]{:S(2)}) copy-start(f32[128,256]{1,0:T(8,128)} %density_ref.1) | copy-start | bytes 393220
  0.9 0.7 %copy-start.1 = (s32[2,4]{1,0:T(2,128)S(1)}, s32[2,4]{1,0:T(2,128)}, u32[]{:S(2)}) copy-start(s32[2,4]{1,0:T(2,128)} %pattern_ref.1) | copy-start | bytes 100

commit v2 on v1

v2 whole, which is shorter than its diff:
```python
import functools

import jax
import jax.numpy as jnp
from jax import lax
from jax.experimental import pallas as pl
from jax.experimental.pallas import tpu as pltpu
from jax.sharding import PartitionSpec as P

ITERS = 2
PIECES = 2
NEAR = 2
MESH = pl.DeviceIdType.MESH


def split(x):
    high = x.astype(jnp.bfloat16)
    low = (x - high.astype(jnp.float32)).astype(jnp.bfloat16)
    return high, low


def flip(index, mask):
    bit = 1
    while bit <= mask:
        if mask & bit:
            index = index + bit * (1 - 2 * lax.rem(index // bit, 2))
        bit *= 2
    return index


def kernel(nrow, ncol, pattern_ref, density_ref, out_ref, rowp, cols, srow, bh, bl, acc, mask,
           zs, zr, cs, cr, ss, sr):
    h, w = density_ref.shape
    pr, pc = pattern_ref.shape
    plane = nrow // 2
    r, z = lax.axis_index("row"), lax.axis_index("col")
    core = lax.rem(r, 2)
    chip = r // 2
    sib = r + 1 - 2 * core
    hp = h // PIECES

    barrier = pltpu.get_barrier_semaphore()
    hops = sorted({d % ncol for near in range(1, NEAR + 1) for d in (near, -near)} - {0})
    greet = [(flip(chip, d) * 2 + core, z) for d in range(1, plane)] + [(sib, z)]
    greet += [(r, lax.rem(z + d, ncol)) for d in hops]
    for device in greet:
        pl.semaphore_signal(barrier, inc=1, device_id=device, device_id_type=MESH)

    lane_block = lax.broadcasted_iota(jnp.int32, (h // pr, w), 1) // (w // pc)
    for i in range(pr):
        band = jnp.zeros((h // pr, w), jnp.float32)
        for j in range(pc):
            band = jnp.where(lane_block == j, pattern_ref[i, j].astype(jnp.float32), band)
        mask[i * (h // pr):(i + 1) * (h // pr), :] = band

    def rows_of(owner, p):
        return pl.ds(pl.multiple_of(owner * h + p * hp, hp), hp)

    def part(p):
        return pl.ds(p * hp, hp)

    rowp[0, z] = density_ref[...]
    cols[0, pl.ds(pl.multiple_of(r * h, h), h), :] = density_ref[...]
    acc[...] = jnp.zeros_like(acc)
    pl.semaphore_wait(barrier, len(greet))

    def remote(ref, send, recv, device):
        return pltpu.make_async_remote_copy(
            src_ref=ref, dst_ref=ref, send_sem=send, recv_sem=recv, device_id=device, device_id_type=MESH)

    def over(low, high, body):
        if ncol <= 4:
            for s in range(low, high):
                body(s)
        else:
            lax.fori_loop(low, high, lambda s, c: (body(s), c)[1], 0)

    def zsend(buf, ph, p, way, s, act, near):
        sign = 1 - 2 * way
        back = 0 if near else s - 1
        ahead = s if near else 1
        block, to = z - sign * back, z + sign * ahead

        @pl.when((block >= 0) & (block <= ncol - 1) & (to >= 0) & (to <= ncol - 1))
        def _():
            copy = remote(buf.at[block, part(p)], zs.at[ph, p, way, s - 1], zr.at[ph, p, way, s - 1], (r, to))
            copy.start() if act == "start" else copy.wait_send()

    def zown(buf, ph, p):
        for s in range(min(NEAR, ncol - 1), 0, -1):
            for way in (0, 1):
                zsend(buf, ph, p, way, s, "start", True)

    def arrive(buf, ph, p, s, passes):
        for way in (0, 1):
            sign = 1 - 2 * way
            block = z - sign * s

            @pl.when((block >= 0) & (block <= ncol - 1))
            def _():
                remote(buf.at[block, part(p)], zs.at[ph, p, way, s - 1], zr.at[ph, p, way, s - 1],
                       (r, z - sign)).wait_recv()
            if passes:
                zsend(buf, ph, p, way, s + 1, "start", False)

    def colcopy(it, p, d, owner, device):
        return remote(cols.at[it, rows_of(owner, p)], cs.at[it, p, d], cr.at[it, p, d], (device, z))

    def sibcopy(it, p, d, owner):
        return remote(cols.at[it, rows_of(owner, p)], ss.at[it, p, d], sr.at[it, p, d], (sib, z))

    def chunk(buf, it, p, j, fresh):
        rows = pl.ds(pl.multiple_of(j * w, w), w)
        if fresh:
            bhigh, blow = split(cols[it, rows, :])
            bh[rows, :] = bhigh
            bl[rows, :] = blow
        else:
            bhigh, blow = bh[rows, :], bl[rows, :]
        ahigh, alow = split(buf[j, part(p), :])
        both = jnp.concatenate([ahigh, alow], axis=0)
        prod = jnp.dot(both, bhigh, preferred_element_type=jnp.float32)
        rest = jnp.dot(ahigh, blow, preferred_element_type=jnp.float32)
        acc[part(p), :] += prod[:hp] + (prod[hp:] + rest)

    def compute(buf, it, p, s, fresh):
        @pl.when(z - s >= 0)
        def _():
            chunk(buf, it, p, z - s, fresh)

        @pl.when(z + s <= ncol - 1)
        def _():
            chunk(buf, it, p, z + s, fresh)

    def finish(buf, ph, it, p, fresh):
        for s in range(1, min(NEAR, ncol - 1) + 1):
            if s < NEAR:
                arrive(buf, ph, p, s, False)
            compute(buf, it, p, s, fresh)

        def far(s):
            arrive(buf, ph, p, s, True)
            compute(buf, it, p, s, fresh)

        over(NEAR + 1, ncol, far)

    def begin(it, p):
        zown(rowp.at[it], 2 * it, p)
        for d in range(1, plane):
            colcopy(it, p, d, r, flip(chip, d) * 2 + core).start()
        sibcopy(it, p, 0, r).start()

    for p in range(PIECES):
        begin(0, p)
    for it in range(ITERS):
        cur, sq = rowp.at[it], srow.at[it]
        pa, pb = 2 * it, 2 * it + 1
        for p in range(PIECES):
            arrive(cur, pa, p, NEAR, True)
            for d in range(1, plane):
                peer = flip(chip, d) * 2 + core
                colcopy(it, p, d, peer, peer).wait_recv()
                sibcopy(it, p, d, peer).start()
        for p in range(PIECES):
            for d in range(plane):
                sibcopy(it, p, d, flip(chip, d) * 2 + 1 - core).wait_recv()
        for p in range(PIECES):
            chunk(cur, it, p, z, p == 0)
            finish(cur, pa, it, p, p == 0)
            sq[z, part(p), :] = acc[part(p), :] * mask[part(p), :]
            acc[part(p), :] = jnp.zeros((hp, w), jnp.float32)
            zown(sq, pb, p)
        for p in range(PIECES):
            chunk(sq, it, p, z, False)
            arrive(sq, pb, p, NEAR, True)
        for p in range(PIECES):
            finish(sq, pb, it, p, False)
            result = 3.0 * sq[z, part(p), :] - 2.0 * (mask[part(p), :] * acc[part(p), :])
            if it + 1 < ITERS:
                acc[part(p), :] = jnp.zeros((hp, w), jnp.float32)
                rowp[it + 1, z, part(p), :] = result
                cols[it + 1, rows_of(r, p), :] = result
                begin(it + 1, p)
            else:
                out_ref[part(p), :] = result

    for it in range(ITERS):
        for p in range(PIECES):
            for buf, ph in ((rowp.at[it], 2 * it), (srow.at[it], 2 * it + 1)):
                for s in range(1, min(NEAR, ncol - 1) + 1):
                    for way in (0, 1):
                        zsend(buf, ph, p, way, s, "wait", True)

                def sent(s):
                    for way in (0, 1):
                        zsend(buf, ph, p, way, s, "wait", False)

                over(NEAR + 1, ncol, sent)
            for d in range(plane):
                peer = flip(chip, d) * 2 + core
                if d:
                    colcopy(it, p, d, r, peer).wait_send()
                sibcopy(it, p, d, peer).wait_send()


def solution(mesh):
    nrow, ncol = mesh.shape["row"], mesh.shape["col"]

    def per_device(density, pattern):
        h, w = density.shape
        n = nrow * h
        f32 = jnp.float32
        dma = pltpu.SemaphoreType.DMA
        return pl.pallas_call(
            functools.partial(kernel, nrow, ncol),
            out_shape=jax.ShapeDtypeStruct((h, w), f32),
            in_specs=[pl.BlockSpec(memory_space=pltpu.SMEM), pl.BlockSpec(memory_space=pltpu.VMEM)],
            out_specs=pl.BlockSpec(memory_space=pltpu.VMEM),
            scratch_shapes=[
                pltpu.VMEM((ITERS, ncol, h, w), f32),
                pltpu.VMEM((ITERS, n, w), f32),
                pltpu.VMEM((ITERS, ncol, h, w), f32),
                pltpu.VMEM((n, w), jnp.bfloat16),
                pltpu.VMEM((n, w), jnp.bfloat16),
                pltpu.VMEM((h, w), f32),
                pltpu.VMEM((h, w), f32),
                dma((2 * ITERS, PIECES, 2, ncol)),
                dma((2 * ITERS, PIECES, 2, ncol)),
                dma((ITERS, PIECES, nrow // 2)),
                dma((ITERS, PIECES, nrow // 2)),
                dma((ITERS, PIECES, nrow // 2)),
                dma((ITERS, PIECES, nrow // 2)),
            ],
            compiler_params=pltpu.CompilerParams(
                collective_id=0, has_side_effects=True, vmem_limit_bytes=40 * 1024 * 1024),
            cost_estimate=pl.CostEstimate(
                flops=12 * ITERS * h * n * w, bytes_accessed=8 * h * w, transcendentals=0),
        )(pattern, density)

    return jax.shard_map(
        per_device,
        mesh=mesh,
        in_specs=(P("row", "col"), P("row", "col")),
        out_specs=P("row", "col"),
        check_vma=False,
    )
```

time: 60.9 us -> 49.8 us (0.82)
  Pallas kernels: 58.5 us -> 47.4 us
    pallas_call x1, Pallas kernels: 58.5 us -> 47.4 us  [per_device(): pl.pallas_call(functools.partial(kernel, nrow, ncol), out_shape=jax.Shape...]
where the time goes in v2:
time: 49.8 us; the launch traced here: 49.6 us
  Pallas kernels  47.4 us (95%)
  local copies, waits for them, and re-layouts  2.24 us (4%)
    pallas_call x1, Pallas kernels, per_device(): pl.pallas_call(functools.partial(kernel, nrow, ncol), out_shape=jax.Shape...  47.4 us
    unnamed x5, local copies, waits for them, and re-layouts  2.24 us

profile of v2, /device:TPU:0, one launch (start us, length us, event | category | flops | bytes accessed | tf_op | source)
XLA Modules:
  0.0 49.6 jit_solution(17912393376635046771)
XLA Ops:
  0.0 0.0 copy-start
  0.0 0.9 %copy-done = f32[128,256]{1,0:T(8,128)S(1)} copy-done((f32[128,256]{1,0:T(8,128)S(1)}, f32[128,256]{1,0:T(8,128)}, u32[]{:S(2)}) %copy-start) | copy-done | bytes 131096
  0.9 0.0 copy-start.1
  0.9 0.7 %copy-done.1 = s32[2,4]{1,0:T(2,128)S(1)} copy-done((s32[2,4]{1,0:T(2,128)S(1)}, s32[2,4]{1,0:T(2,128)}, u32[]{:S(2)}) %copy-start.1) | copy-done | bytes 56
  1.6 47.4 %shard_map.28 = f32[128,256]{1,0:T(8,128)S(1)} custom-call(s32[2,4]{1,0:T(2,128)S(1)} %copy-done.1, f32[128,256]{1,0:T(8,128)S(1)} %copy-done), custom_call_target="tpu_custom_call" | custom-call | flops 805306368 | bytes 262144 | tf_op jit(solution)/shard_map/pallas_call | solution.py:214
  49.0 0.7 %copy.4 = f32[128,256]{1,0:T(8,128)} copy(f32[128,256]{1,0:T(8,128)S(1)} %shard_map.28) | data formatting | bytes 262144
Async XLA Ops:
  0.0 0.9 %copy-start = (f32[128,256]{1,0:T(8,128)S(1)}, f32[128,256]{1,0:T(8,128)}, u32[]{:S(2)}) copy-start(f32[128,256]{1,0:T(8,128)} %density_ref.1) | copy-start | bytes 393220
  0.9 0.7 %copy-start.1 = (s32[2,4]{1,0:T(2,128)S(1)}, s32[2,4]{1,0:T(2,128)}, u32[]{:S(2)}) copy-start(s32[2,4]{1,0:T(2,128)} %pattern_ref.1) | copy-start | bytes 100

commit v3 on v2

--- a/solution.py
+++ b/solution.py
@@ -28,10 +28,10 @@
     return index
 
 
-def kernel(nrow, ncol, pattern_ref, density_ref, out_ref, rowp, cols, srow, bh, bl, acc, mask,
+def kernel(nrow, ncol, pattern_hbm, density_ref, out_ref, pattern_ref, local, rowp, cols, srow, bh, bl, acc, mask,
            zs, zr, cs, cr, ss, sr):
     h, w = density_ref.shape
-    pr, pc = pattern_ref.shape
+    pr, pc = pattern_hbm.shape
     plane = nrow // 2
     r, z = lax.axis_index("row"), lax.axis_index("col")
     core = lax.rem(r, 2)
@@ -39,6 +39,10 @@
     sib = r + 1 - 2 * core
     hp = h // PIECES
 
+    take_pattern = pltpu.make_async_copy(pattern_hbm, pattern_ref, local.at[0])
+    take_density = pltpu.make_async_copy(density_ref, rowp.at[0, z], local.at[1])
+    take_pattern.start()
+    take_density.start()
     barrier = pltpu.get_barrier_semaphore()
     hops = sorted({d % ncol for near in range(1, NEAR + 1) for d in (near, -near)} - {0})
     greet = [(flip(chip, d) * 2 + core, z) for d in range(1, plane)] + [(sib, z)]
@@ -46,6 +50,7 @@
     for device in greet:
         pl.semaphore_signal(barrier, inc=1, device_id=device, device_id_type=MESH)
 
+    take_pattern.wait()
     lane_block = lax.broadcasted_iota(jnp.int32, (h // pr, w), 1) // (w // pc)
     for i in range(pr):
         band = jnp.zeros((h // pr, w), jnp.float32)
@@ -59,8 +64,8 @@
     def part(p):
         return pl.ds(p * hp, hp)
 
-    rowp[0, z] = density_ref[...]
-    cols[0, pl.ds(pl.multiple_of(r * h, h), h), :] = density_ref[...]
+    take_density.wait()
+    cols[0, pl.ds(pl.multiple_of(r * h, h), h), :] = rowp[0, z]
     acc[...] = jnp.zeros_like(acc)
     pl.semaphore_wait(barrier, len(greet))
 
@@ -75,21 +80,33 @@
         else:
             lax.fori_loop(low, high, lambda s, c: (body(s), c)[1], 0)
 
-    def zsend(buf, ph, p, way, s, act, near):
+    def zsend(buf, ph, p, way, s, act, near, only=None):
         sign = 1 - 2 * way
         back = 0 if near else s - 1
         ahead = s if near else 1
         block, to = z - sign * back, z + sign * ahead
 
-        @pl.when((block >= 0) & (block <= ncol - 1) & (to >= 0) & (to <= ncol - 1))
+        inside = (block >= 0) & (block <= ncol - 1) & (to >= 0) & (to <= ncol - 1)
+        if only == "end":
+            inside = (to == (ncol - 1 if way == 0 else 0)) & (block >= 0) & (block <= ncol - 1)
+        elif only == "middle":
+            inside = (to > 0) & (to < ncol - 1)
+
+        @pl.when(inside)
         def _():
             copy = remote(buf.at[block, part(p)], zs.at[ph, p, way, s - 1], zr.at[ph, p, way, s - 1], (r, to))
             copy.start() if act == "start" else copy.wait_send()
 
     def zown(buf, ph, p):
-        for s in range(min(NEAR, ncol - 1), 0, -1):
+        for way in (0, 1):
+            zsend(buf, ph, p, way, 1, "start", True, "end")
+        for s in range(min(NEAR, ncol - 1), 1, -1):
             for way in (0, 1):
                 zsend(buf, ph, p, way, s, "start", True)
+
+    def znear(buf, ph, p):
+        for way in (0, 1):
+            zsend(buf, ph, p, way, 1, "start", True, "middle")
 
     def arrive(buf, ph, p, s, passes):
         for way in (0, 1):
@@ -152,6 +169,8 @@
 
     for p in range(PIECES):
         begin(0, p)
+    for p in range(PIECES):
+        znear(rowp.at[0], 0, p)
     for it in range(ITERS):
         cur, sq = rowp.at[it], srow.at[it]
         pa, pb = 2 * it, 2 * it + 1
@@ -170,6 +189,8 @@
             sq[z, part(p), :] = acc[part(p), :] * mask[part(p), :]
             acc[part(p), :] = jnp.zeros((hp, w), jnp.float32)
             zown(sq, pb, p)
+        for p in range(PIECES):
+            znear(sq, pb, p)
         for p in range(PIECES):
             chunk(sq, it, p, z, False)
             arrive(sq, pb, p, NEAR, True)
@@ -183,6 +204,9 @@
                 begin(it + 1, p)
             else:
                 out_ref[part(p), :] = result
+        if it + 1 < ITERS:
+            for p in range(PIECES):
+                znear(rowp.at[it + 1], pa + 2, p)
 
     for it in range(ITERS):
         for p in range(PIECES):
@@ -214,9 +238,11 @@
         return pl.pallas_call(
             functools.partial(kernel, nrow, ncol),
             out_shape=jax.ShapeDtypeStruct((h, w), f32),
-            in_specs=[pl.BlockSpec(memory_space=pltpu.SMEM), pl.BlockSpec(memory_space=pltpu.VMEM)],
+            in_specs=[pl.BlockSpec(memory_space=pltpu.HBM), pl.BlockSpec(memory_space=pltpu.HBM)],
             out_specs=pl.BlockSpec(memory_space=pltpu.VMEM),
             scratch_shapes=[
+                pltpu.SMEM(pattern.shape, jnp.int32),
+                dma((2,)),
                 pltpu.VMEM((ITERS, ncol, h, w), f32),
                 pltpu.VMEM((ITERS, n, w), f32),
                 pltpu.VMEM((ITERS, ncol, h, w), f32),
@@ -232,7 +258,7 @@
                 dma((ITERS, PIECES, nrow // 2)),
             ],
             compiler_params=pltpu.CompilerParams(
-                collective_id=0, has_side_effects=True, vmem_limit_bytes=40 * 1024 * 1024),
+                collective_id=0, has_side_effects=True, vmem_limit_bytes=60 * 1024 * 1024),
             cost_estimate=pl.CostEstimate(
                 flops=12 * ITERS * h * n * w, bytes_accessed=8 * h * w, transcendentals=0),
         )(pattern, density)

time: 49.8 us -> 48.9 us (0.982)
  local copies, waits for them, and re-layouts: 2.24 us -> 1.57 us
    unnamed x5 -> x1, local copies, waits for them, and re-layouts: 2.24 us -> 1.57 us
where the time goes in v3:
time: 48.9 us; the launch traced here: 48.7 us
  Pallas kernels  47.1 us (96%)
  local copies, waits for them, and re-layouts  1.57 us (3%)
    pallas_call x1, Pallas kernels, per_device(): pl.pallas_call(functools.partial(kernel, nrow, ncol), out_shape=jax.Shape...  47.1 us
    unnamed x1, local copies, waits for them, and re-layouts  1.57 us

profile of v3, /device:TPU:0, one launch (start us, length us, event | category | flops | bytes accessed | tf_op | source)
XLA Modules:
  0.0 48.7 jit_solution(5210993370549946642)
XLA Ops:
  0.0 47.1 %shard_map.28 = f32[128,256]{1,0:T(8,128)} custom-call(s32[2,4]{1,0:T(2,128)} %pattern_hbm.1, f32[128,256]{1,0:T(8,128)} %density_ref.1), custom_call_target="tpu_custom_call" | custom-call | flops 805306368 | bytes 262144 | tf_op jit(solution)/shard_map/pallas_call | solution.py:238
  47.2 1.6 %copy.4 = f32[128,256]{1,0:T(8,128)} copy(f32[128,256]{1,0:T(8,128)} %shard_map.28) | data formatting | bytes 262144

commit v4 on v3

--- a/solution.py
+++ b/solution.py
@@ -162,11 +162,14 @@
         over(NEAR + 1, ncol, far)
 
     def begin(it, p):
-        zown(rowp.at[it], 2 * it, p)
+        if it:
+            zown(rowp.at[it], 2 * it, p)
         for d in range(1, plane):
             colcopy(it, p, d, r, flip(chip, d) * 2 + core).start()
         sibcopy(it, p, 0, r).start()
 
+    for p in range(PIECES):
+        zown(rowp.at[0], 0, p)
     for p in range(PIECES):
         begin(0, p)
     for p in range(PIECES):

time: 48.9 us -> 48.9 us (level)
  no operation moved by 1% of the time
where the time goes in v4:
time: 48.9 us; the launch traced here: 48.7 us
  Pallas kernels  47.1 us (96%)
  local copies, waits for them, and re-layouts  1.57 us (3%)
    pallas_call x1, Pallas kernels, per_device(): pl.pallas_call(functools.partial(kernel, nrow, ncol), out_shape=jax.Shape...  47.1 us
    unnamed x1, local copies, waits for them, and re-layouts  1.57 us

profile of v4, /device:TPU:0, one launch (start us, length us, event | category | flops | bytes accessed | tf_op | source)
XLA Modules:
  0.0 48.7 jit_solution(431724040762132405)
XLA Ops:
  0.0 47.1 %shard_map.28 = f32[128,256]{1,0:T(8,128)} custom-call(s32[2,4]{1,0:T(2,128)} %pattern_hbm.1, f32[128,256]{1,0:T(8,128)} %density_ref.1), custom_call_target="tpu_custom_call" | custom-call | flops 805306368 | bytes 262144 | tf_op jit(solution)/shard_map/pallas_call | solution.py:241
  47.2 1.6 %copy.4 = f32[128,256]{1,0:T(8,128)} copy(f32[128,256]{1,0:T(8,128)} %shard_map.28) | data formatting | bytes 262144
